TPU v7x, 32 devices: a whole 2x2x4 slice. The times are simulated.
32 devices in a mesh: groups: 2 (over y), chan: 8 (over z, x), tm: 2 (over core).
Axes of the slice: x: 2, y: 2, z: 4, core: 2. Of those that a mesh axis runs over, the one named last changes fastest.
Arguments:
- strain: bfloat16 [1024, 16384], P(('groups', 'chan'), 'tm'), parts along dimension 0, may hold values from -500 to 500, as said below
- taps: float32 [64], replicated, may hold values from -0.75 to 0.75
- offsets: int32 [16, 2], P(('groups', 'chan')), parts along dimension 0, may hold values from 1 to 4, as said below
- valid: int32 [16], P(('groups', 'chan')), parts along dimension 0, may hold values from 32 to 64, as said below
Outputs:
- corr: float32 [1024, 2, 512], P(('groups', 'chan'), 'tm'), parts along dimension 0
There are 2 independent parts, one for each index of `groups`. A program takes and returns all parts, laid end to end along the dimension named above; an argument that names none is the same for every part. Nothing has to cross between parts.
Inputs may be any that keep to these rules, and one draw needn't show every extreme that they name: strain samples; scales differ between channels and between stretches of time. The 2 offsets of a block differ from one another; the partner of block b at offset o is block b + o, and a partner past the last block contributes zeros. `valid`: channels of a block at positions from this count on are dead.
All inputs are finite; a program needn't handle non-finite values.
Results may differ from a plain program's by a relative error of at most 0.017.
Values may be sent and summed in bfloat16 or wider, within the bound.
A program may use at most 64 MiB of HBM per device.

v0:
```python
import math

import jax
import jax.numpy as jnp
from jax import lax
from jax.sharding import PartitionSpec as P

NFFT = 1024
LAGS = 512
MAXOFF = 4


def passed_along(value, axis, steps):
    count = lax.axis_size(axis)
    first, last = (max(0, -steps), min(count, count - steps))
    return lax.ppermute(value, axis, [(source, source + steps) for source in range(first, last)])


def fourier_table(fft_len, bins):
    sample_idx = lax.broadcasted_iota(jnp.int32, (fft_len, bins), 0)
    bin_idx = lax.broadcasted_iota(jnp.int32, (fft_len, bins), 1)
    phase = (sample_idx * bin_idx % fft_len).astype(jnp.float32) * (2.0 * math.pi / fft_len)
    return jnp.concatenate([jnp.cos(phase), -jnp.sin(phase)], axis=1).astype(jnp.bfloat16)


def lag_table(fft_len, bins, lag_count):
    bin_idx = lax.broadcasted_iota(jnp.int32, (bins, lag_count), 0)
    lag_idx = lax.broadcasted_iota(jnp.int32, (bins, lag_count), 1) - lag_count // 2
    phase = (bin_idx * lag_idx % fft_len).astype(jnp.float32) * (2.0 * math.pi / fft_len)
    return jnp.concatenate([jnp.cos(phase), -jnp.sin(phase)], axis=0)


def fir_matrix(taps, block_len):
    ntaps = taps.shape[0]
    rows = block_len + ntaps
    row_idx = lax.broadcasted_iota(jnp.int32, (rows, block_len), 0)
    col_idx = lax.broadcasted_iota(jnp.int32, (rows, block_len), 1)
    tap_idx = col_idx + ntaps - row_idx
    onehot = (tap_idx[:, :, None] == lax.broadcasted_iota(jnp.int32, (1, 1, ntaps), 2)).astype(
        jnp.float32
    )
    return jnp.dot(
        onehot.reshape(rows * block_len, ntaps), taps, precision=lax.Precision.HIGHEST
    ).reshape(rows, block_len)


def whiten(spectra, live, bins):
    real_part = spectra[..., :bins]
    imag_part = spectra[..., bins:]
    energy = real_part * real_part + imag_part * imag_part
    power = jnp.mean(energy, axis=-1, keepdims=True) + 1e-06
    factor = live / jnp.sqrt(energy + 0.1 * power)
    return jnp.concatenate([real_part * factor, imag_part * factor], axis=-1).astype(jnp.bfloat16)


def cross_spectrum(own, partner, bins):
    own_r = own[..., :bins]
    own_i = own[..., bins:]
    part_r = partner[..., :bins]
    part_i = partner[..., bins:]

    def contract(left, right):
        return jnp.einsum("scf,scf->cf", left, right, preferred_element_type=jnp.float32)

    cross_r = contract(own_r, part_r) + contract(own_i, part_i)
    cross_i = contract(own_i, part_r) - contract(own_r, part_i)
    return jnp.concatenate([cross_r, cross_i], axis=-1)


def on_device(strain, taps, offsets, valid):
    channels, length = strain.shape
    ntaps = taps.shape[0]
    fft_len = NFFT
    bins = fft_len // 2
    block_len = min(128, fft_len)
    history = passed_along(strain[:, length - ntaps :], "tm", 1)
    padded = jnp.concatenate([history, strain], axis=1)
    nblocks = length // block_len
    lower = padded[:, :length].reshape(channels, nblocks, block_len)
    upper = strain.reshape(channels, nblocks, block_len)[:, :, block_len - ntaps :]
    window = jnp.concatenate([lower, upper], axis=2)
    fir_full = fir_matrix(taps, block_len)
    fir_high = fir_full.astype(jnp.bfloat16)
    fir_low = (fir_full - fir_high.astype(jnp.float32)).astype(jnp.bfloat16)
    filtered = jnp.einsum("cjw,ws->cjs", window, fir_high, preferred_element_type=jnp.float32)
    filtered = filtered + jnp.einsum(
        "cjw,ws->cjs", window, fir_low, preferred_element_type=jnp.float32
    )
    rounded = filtered.reshape(channels, length).astype(jnp.bfloat16)
    segments = length // fft_len
    frames = rounded.reshape(channels, segments, fft_len)
    spectra = jnp.einsum(
        "csn,nf->scf", frames, fourier_table(fft_len, bins), preferred_element_type=jnp.float32
    )
    live = (lax.broadcasted_iota(jnp.int32, (1, channels, 1), 1) < valid[0]).astype(jnp.float32)
    panel = whiten(spectra, live, bins)
    received = []
    for distance in range(1, MAXOFF + 1):
        received.append(passed_along(panel, "chan", -distance))
    stacked = jnp.stack(received, axis=0)
    pairs = offsets.shape[1]
    terms = []
    for pair_slot in range(pairs):
        partner = lax.dynamic_index_in_dim(stacked, offsets[0, pair_slot] - 1, 0, keepdims=False)
        terms.append(cross_spectrum(panel, partner, bins))
    cross = jnp.stack(terms, axis=1)
    inverse = lag_table(fft_len, bins, LAGS)
    denominator = math.sqrt(bins * segments * lax.axis_size("tm"))
    summed = lax.psum_scatter(
        cross.astype(jnp.bfloat16), "tm", scatter_dimension=1, tiled=True
    ).astype(jnp.float32)
    corr = jnp.einsum("cjf,fl->cjl", summed, inverse, precision=lax.Precision.HIGHEST) / denominator
    return corr


def solution(mesh):
    in_specs = (
        P(("groups", "chan"), "tm"),
        P(),
        P(("groups", "chan"), None),
        P(("groups", "chan")),
    )
    out_specs = P(("groups", "chan"), "tm", None)
    return jax.shard_map(
        on_device, mesh=mesh, in_specs=in_specs, out_specs=out_specs, check_vma=False
    )
```

profile of v0, /device:TPU:0, one launch (start us, length us, event | category | flops | bytes accessed | tf_op | source)
XLA Modules:
  0.0 188.8 jit_solution(16484655792350432286)
XLA Ops:
  6.5 0.0 copy-start
  6.5 0.0 copy-start.1
  6.5 0.0 reduce-scatter.2.cloned.1.call-start
  6.5 0.9 slice.41
  7.4 2.3 %collective-permute-start = (bf16[64,64]{1,0:T(8,128)(2,1)S(1)}, bf16[64,64]{1,0:T(8,128)(2,1)S(1)}, u32[]{:S(2)}, u32[]{:S(2)}) collective-permute-start(bf16[64,64]{1,0:T(8,128)(2,1)S(1)} %slice.41), channel_id=1, source_target_pairs={{0,1},{2,3},{4,5},{6,7},{8,9},{10,11},{12,13},{14,15},{16,17},{18,... | collective-permute-start | bytes 24584 | tf_op jit(solution)/shard_map/ppermute | solution.py:16
  9.8 8.5 %negate_convert_fusion = (bf16[1024,512]{1,0:T(8,128)(2,1)S(1)}, bf16[1024,512]{1,0:T(8,128)(2,1)S(1)}) fusion(), kind=kLoop, calls=%fused_computation.20 | loop fusion | flops 8912896 | bytes 2097152 | tf_op jit(solution)/shard_map/convert.11
  19.0 0.0 copy-done
  19.0 2.0 %fusion = f32[1,192,128]{2,0,1:T(1,128)S(1)} fusion(s32[192,128]{1,0:T(8,128)S(1)} %iota_subtract_fusion, f32[64]{0:T(128)S(1)} %copy-done), kind=kOutput, calls=%fused_computation.1 | convolution fusion | flops 20447232 | bytes 196864 | tf_op jit(solution)/shard_map/dot_general | solution.py:42
  21.0 0.0 copy-done.1
  21.0 0.3 copy.67
  21.3 0.4 slice.54
  21.7 0.0 collective-permute-done
  21.7 0.4 fusion.34
  22.1 0.3 copy.66
  22.4 0.7 fusion.16
  23.1 0.7 add_convert_fusion
  23.8 1.3 convert_element_type.44
  25.1 2.6 %fusion.15 = f32[8,64,1024]{2,1,0:T(8,128)S(1)} fusion(bf16[1024,512]{1,0:T(8,128)(2,1)S(1)} %get-tuple-element.29, bf16[1024,512]{1,0:T(8,128)(2,1)S(1)} %get-tuple-element.30, bf16[64,8,1024]{2,1,0:T(8,128)(2,1)} %convert_element_type.44), kind=kOutput, calls=%fused_computation.33 | convolution fusion | flops 1077936128 | bytes 5242880 | tf_op jit(solution)/shard_map/csn,nf->scf/dot_general | solution.py:92
  27.7 0.2 fusion.51
  27.9 0.0 copy-start.2
  27.9 0.5 multiply_convert_fusion.1
  28.4 0.1 pad_maximum_fusion.5
  28.6 1.3 collective-permute-start.1
  29.9 1.3 collective-permute-start.2
  31.2 1.3 collective-permute-start.3
  32.5 1.5 collective-permute-start.4
  33.9 0.0 copy-done.2
  34.0 0.6 fusion.52
  36.9 18.6 %collective-permute-done.1 = bf16[8,64,1024]{2,1,0:T(8,128)(2,1)S(1)} collective-permute-done((bf16[8,64,1024]{2,1,0:T(8,128)(2,1)S(1)}, bf16[8,64,1024]{2,1,0:T(8,128)(2,1)S(1)}, u32[]{:S(2)}, u32[]{:S(2)}) %collective-permute-start.1) | collective-permute-done | bytes 1048608 | tf_op jit(solution)/shard_map/ppermute | solution.py:16
  55.5 24.3 %collective-permute-done.2 = bf16[8,64,1024]{2,1,0:T(8,128)(2,1)} collective-permute-done((bf16[8,64,1024]{2,1,0:T(8,128)(2,1)S(1)}, bf16[8,64,1024]{2,1,0:T(8,128)(2,1)}, u32[]{:S(2)}, u32[]{:S(2)}) %collective-permute-start.2) | collective-permute-done | bytes 1048608 | tf_op jit(solution)/shard_map/ppermute | solution.py:16
  79.8 2.0 %collective-permute-done.3 = bf16[8,64,1024]{2,1,0:T(8,128)(2,1)} collective-permute-done((bf16[8,64,1024]{2,1,0:T(8,128)(2,1)S(1)}, bf16[8,64,1024]{2,1,0:T(8,128)(2,1)}, u32[]{:S(2)}, u32[]{:S(2)}) %collective-permute-start.3) | collective-permute-done | bytes 1048608 | tf_op jit(solution)/shard_map/ppermute | solution.py:16
  81.8 88.3 %collective-permute-done.4 = bf16[8,64,1024]{2,1,0:T(8,128)(2,1)} collective-permute-done((bf16[8,64,1024]{2,1,0:T(8,128)(2,1)S(1)}, bf16[8,64,1024]{2,1,0:T(8,128)(2,1)}, u32[]{:S(2)}, u32[]{:S(2)}) %collective-permute-start.4) | collective-permute-done | bytes 1048608 | tf_op jit(solution)/shard_map/ppermute | solution.py:16
  170.1 2.1 %pad_maximum_fusion = bf16[4,8,64,1024]{3,2,1,0:T(8,128)(2,1)S(1)} fusion(bf16[1,8,64,1024]{3,2,1,0:T(8,128)(2,1)} %bitcast.27, bf16[1,8,64,1024]{3,2,1,0:T(8,128)(2,1)} %bitcast.26, bf16[1,8,64,1024]{3,2,1,0:T(8,128)(2,1)} %bitcast.25, bf16[1,8,64,1024]{3,2,1,0:T(8,128)(2,1)S(1)} %bitcast.94), kind=kLoop, calls=%fused_computation.2 | loop fusion | flops 6291456 | bytes 8388608 | tf_op jit(solution)/shard_map/stack | solution.py:100
  172.3 0.2 dynamic-slice_bitcast_fusion.1
  172.5 0.8 fusion.32
  173.4 0.7 pad_maximum_fusion.6
  174.2 0.0 reduce-scatter.2.cloned.1.call-update
  174.2 4.1 %fusion.39 = (f32[512,512]{1,0:T(8,128)S(1)}, f32[512,512]{1,0:T(8,128)S(1)}) fusion(s32[512]{0:T(512)S(1)} %iota_add_fusion), kind=kLoop, calls=%fused_computation.69 | loop fusion | flops 3932160 | bytes 2099200 | tf_op jit(solution)/shard_map/cos | solution.py:30
  178.3 1.0 reduce-scatter.2.cloned.1.call-done
  179.3 1.8 fusion.20
  181.1 0.8 copy.8
  (11 shorter events, 0.1 us)
Async XLA Ops:
  6.5 12.5 %copy-start = (f32[64]{0:T(128)S(1)}, f32[64]{0:T(128)}, u32[]{:S(2)}) copy-start(f32[64]{0:T(128)} %param.5) | copy-start | bytes 772
  6.5 14.5 %copy-start.1 = (bf16[64,8192]{1,0:T(8,128)(2,1)S(1)}, bf16[64,8192]{1,0:T(8,128)(2,1)}, u32[]{:S(2)}) copy-start(bf16[64,8192]{1,0:T(8,128)(2,1)} %param.4) | copy-start | bytes 3145732
  6.5 172.8 %reduce-scatter.2.cloned.1.call-start = ((), (), s32[]{:S(2)}) async-start(), calls=%async_computation.1 | async-start | bytes 393216 | tf_op jit(solution)/shard_map/reduce_scatter | solution.py:109
  7.4 14.3 %collective-permute-start = (bf16[64,64]{1,0:T(8,128)(2,1)S(1)}, bf16[64,64]{1,0:T(8,128)(2,1)S(1)}, u32[]{:S(2)}, u32[]{:S(2)}) collective-permute-start(bf16[64,64]{1,0:T(8,128)(2,1)S(1)} %slice.41), channel_id=1, source_target_pairs={{0,1},{2,3},{4,5},{6,7},{8,9},{10,11},{12,13},{14,15},{16,17},{18,... | collective-permute-start | bytes 24584 | tf_op jit(solution)/shard_map/ppermute | solution.py:16
  27.9 6.0 %copy-start.2 = (s32[1,2]{1,0:T(1,128)S(1)}, s32[1,2]{1,0:T(1,128)}, u32[]{:S(2)}) copy-start(s32[1,2]{1,0:T(1,128)} %param.6) | copy-start | bytes 28
  28.6 26.9 %collective-permute-start.1 = (bf16[8,64,1024]{2,1,0:T(8,128)(2,1)S(1)}, bf16[8,64,1024]{2,1,0:T(8,128)(2,1)S(1)}, u32[]{:S(2)}, u32[]{:S(2)}) collective-permute-start(bf16[8,64,1024]{2,1,0:T(8,128)(2,1)S(1)} %pad_maximum_fusion.5), channel_id=1, source_target_pairs={{2,0},{4,2},{6,4},{8,6},{10,8},{12,10},{14,12},{3,1},{5,3},{7,5},{... | collective-permute-start | bytes 3145736 | tf_op jit(solution)/shard_map/ppermute | solution.py:16
  29.9 49.9 %collective-permute-start.2 = (bf16[8,64,1024]{2,1,0:T(8,128)(2,1)S(1)}, bf16[8,64,1024]{2,1,0:T(8,128)(2,1)}, u32[]{:S(2)}, u32[]{:S(2)}) collective-permute-start(bf16[8,64,1024]{2,1,0:T(8,128)(2,1)S(1)} %pad_maximum_fusion.5), channel_id=1, source_target_pairs={{4,0},{6,2},{8,4},{10,6},{12,8},{14,10},{5,1},{7,3},{9,5},{11,7},{... | collective-permute-start | bytes 3145736 | tf_op jit(solution)/shard_map/ppermute | solution.py:16
  31.2 50.7 %collective-permute-start.3 = (bf16[8,64,1024]{2,1,0:T(8,128)(2,1)S(1)}, bf16[8,64,1024]{2,1,0:T(8,128)(2,1)}, u32[]{:S(2)}, u32[]{:S(2)}) collective-permute-start(bf16[8,64,1024]{2,1,0:T(8,128)(2,1)S(1)} %pad_maximum_fusion.5), channel_id=1, source_target_pairs={{6,0},{8,2},{10,4},{12,6},{14,8},{7,1},{9,3},{11,5},{13,7},{15,9},... | collective-permute-start | bytes 3145736 | tf_op jit(solution)/shard_map/ppermute | solution.py:16
  32.5 137.7 %collective-permute-start.4 = (bf16[8,64,1024]{2,1,0:T(8,128)(2,1)S(1)}, bf16[8,64,1024]{2,1,0:T(8,128)(2,1)}, u32[]{:S(2)}, u32[]{:S(2)}) collective-permute-start(bf16[8,64,1024]{2,1,0:T(8,128)(2,1)S(1)} %pad_maximum_fusion.5), channel_id=1, source_target_pairs={{8,0},{10,2},{12,4},{14,6},{9,1},{11,3},{13,5},{15,7},{24,16},{26,... | collective-permute-start | bytes 3145736 | tf_op jit(solution)/shard_map/ppermute | solution.py:16
Sparse Core Ops, SparseCore 0:
  174.3 4.9 reduce-scatter.1
where the time goes:
time: 189 us
  waiting for transfers between devices  134 us (71%)
  other arithmetic  17.6 us (9%)
  between operations  16.7 us (9%)
  matrix products  7.81 us (4%)
  starting transfers between devices  7.7 us (4%)
  local copies, waits for them, and re-layouts  4.71 us (2%)
    ppermute x5, waiting for transfers between devices, passed_along(): lax.ppermute(value, axis, [(source, source + steps) for source in range(f...  133 us
    another operation x5, other arithmetic  8.63 us
    ppermute x5, starting transfers between devices, passed_along(): lax.ppermute(value, axis, [(source, source + steps) for source in range(f...  7.7 us
    cos x1, other arithmetic, lag_table(): return jnp.concatenate([jnp.cos(phase), -jnp.sin(phase)], axis=0)  4.12 us
  transfers between devices with their start and end apart: 6, of which 5 were waited for; matrix products, arithmetic and copies ran while one was open for 8% of the time, Pallas kernels for 0%

commit v1 on v0

--- a/solution.py
+++ b/solution.py
@@ -1,13 +1,316 @@
+import functools
 import math
 
 import jax
 import jax.numpy as jnp
+import numpy as np
 from jax import lax
+from jax.experimental import pallas as pl
+from jax.experimental.pallas import tpu as pltpu
 from jax.sharding import PartitionSpec as P
 
 NFFT = 1024
 LAGS = 512
 MAXOFF = 4
+MESH_ID = pl.DeviceIdType.MESH
+SEGS_PER_CHUNK = 2
+
+
+def host_fourier_table(fft_len, bins):
+    sample_idx = np.arange(fft_len)[:, None]
+    bin_idx = np.arange(bins)[None, :]
+    phase = (2.0 * math.pi / fft_len) * (sample_idx * bin_idx % fft_len)
+    return np.concatenate([np.cos(phase), -np.sin(phase)], axis=1).astype(jnp.bfloat16)
+
+
+def host_lag_table(fft_len, bins, lag_count):
+    bin_idx = np.arange(bins)[:, None]
+    lag_idx = np.arange(lag_count)[None, :] - lag_count // 2
+    phase = (2.0 * math.pi / fft_len) * (bin_idx * lag_idx % fft_len)
+    return np.concatenate([np.cos(phase), -np.sin(phase)], axis=0).astype(jnp.bfloat16)
+
+
+def kernel(
+    blocks,
+    scale,
+    strain_hbm,
+    table_hbm,
+    inverse_hbm,
+    taps_ref,
+    offs_ref,
+    valid_ref,
+    out_ref,
+    strain,
+    table,
+    inverse,
+    history,
+    offs_all,
+    offs_smem,
+    acc,
+    other_send,
+    other_recv,
+    ret_send,
+    *rest,
+):
+    channels, length = strain.shape
+    fft_len = table.shape[0]
+    bins = fft_len // 2
+    segments = length // fft_len
+    nchunks = segments // SEGS_PER_CHUNK
+    positions = channels // blocks
+    send = rest[:nchunks]
+    recv = rest[nchunks : 2 * nchunks]
+    (local_sem, hist_sem, offs_send_sem, offs_recv_sem, send_sem, recv_sem, other_sem,
+     ret_send_sem, ret_recv_sem) = rest[2 * nchunks :]
+
+    me = lax.axis_index("chan")
+    tm = lax.axis_index("tm")
+    steps = range(1, blocks)
+
+    def peer(step):
+        return lax.rem(me + step, blocks)
+
+    strain_copy = pltpu.make_async_copy(strain_hbm, strain, local_sem.at[0])
+    table_copy = pltpu.make_async_copy(table_hbm, table, local_sem.at[1])
+    inverse_copy = pltpu.make_async_copy(inverse_hbm, inverse, local_sem.at[2])
+    strain_copy.start()
+    table_copy.start()
+    inverse_copy.start()
+
+    barrier = pltpu.get_barrier_semaphore()
+    for step in steps:
+        pl.semaphore_signal(barrier, inc=1, device_id={"chan": peer(step)}, device_id_type=MESH_ID)
+    pl.semaphore_signal(barrier, inc=1, device_id={"tm": 1 - tm}, device_id_type=MESH_ID)
+
+    base = jnp.broadcast_to(taps_ref[...], (256, 256))
+    fir_full = pltpu.roll(base, 128, 1, stride=1, stride_axis=0)[:, :128]
+    fir_high = fir_full.astype(jnp.bfloat16)
+    fir_low = (fir_full - fir_high.astype(jnp.float32)).astype(jnp.bfloat16)
+    fir = jnp.concatenate([fir_high, fir_low], axis=1)
+
+    pl.semaphore_wait(barrier, blocks)
+    strain_copy.wait()
+
+    hist_copy = pltpu.make_async_remote_copy(
+        src_ref=strain.at[:, length - 128 :],
+        dst_ref=history,
+        send_sem=hist_sem.at[0],
+        recv_sem=hist_sem.at[1],
+        device_id={"tm": 1 - tm},
+        device_id_type=MESH_ID,
+    )
+
+    @pl.when(tm == 0)
+    def _():
+        hist_copy.start()
+        history[...] = jnp.zeros_like(history)
+
+    offs_copies = []
+    for step in steps:
+        copy = pltpu.make_async_remote_copy(
+            src_ref=offs_ref,
+            dst_ref=offs_all.at[me],
+            send_sem=offs_send_sem.at[step],
+            recv_sem=offs_recv_sem.at[step],
+            device_id={"chan": peer(step)},
+            device_id_type=MESH_ID,
+        )
+        copy.start()
+        offs_copies.append(copy)
+    offs_all[me] = offs_ref[...]
+
+    table_copy.wait()
+    live = lax.broadcasted_iota(jnp.int32, (channels, 1), 0) < valid_ref[0]
+    live = jnp.where(live, 1.0, 0.0).astype(jnp.float32)
+    live = jnp.concatenate([live] * SEGS_PER_CHUNK, axis=0)
+
+    chunk_order = list(range(1, nchunks)) + [0]
+    copies = {}
+    for chunk in chunk_order:
+        first = chunk * SEGS_PER_CHUNK
+        windows = []
+        for j in range(first * 8, (first + SEGS_PER_CHUNK) * 8):
+            if j == 0:
+
+                @pl.when(tm == 1)
+                def _():
+                    hist_copy.wait_recv()
+
+                windows.append(jnp.concatenate([history[...], strain[:, :128]], axis=1))
+            else:
+                windows.append(strain[:, 128 * (j - 1) : 128 * (j + 1)])
+        window = jnp.concatenate(windows, axis=0)
+        both = jnp.dot(window, fir, preferred_element_type=jnp.float32)
+        rounded = (both[:, :128] + both[:, 128:]).astype(jnp.bfloat16)
+        frames = jnp.concatenate(
+            [
+                jnp.concatenate(
+                    [
+                        rounded[(seg * 8 + j) * channels : (seg * 8 + j + 1) * channels]
+                        for j in range(8)
+                    ],
+                    axis=1,
+                )
+                for seg in range(SEGS_PER_CHUNK)
+            ],
+            axis=0,
+        )
+        spectra = jnp.dot(frames, table[...], preferred_element_type=jnp.float32)
+        real_part = spectra[:, :bins]
+        imag_part = spectra[:, bins:]
+        energy = real_part * real_part + imag_part * imag_part
+        power = jnp.mean(energy, axis=1, keepdims=True) + 1e-06
+        factor = live * lax.rsqrt(energy + 0.1 * power)
+        white_r = real_part * factor
+        white_i = imag_part * factor
+        for block in range(blocks):
+            for part, half in ((white_r, 0), (white_i, 1)):
+                rows = jnp.concatenate(
+                    [
+                        part[seg * channels + block * positions :][:positions]
+                        for seg in range(SEGS_PER_CHUNK)
+                    ],
+                    axis=0,
+                )
+                send[chunk][block, :, half * bins : (half + 1) * bins] = rows.astype(jnp.bfloat16)
+        for step in steps:
+            copy = pltpu.make_async_remote_copy(
+                src_ref=send[chunk].at[peer(step)],
+                dst_ref=recv[chunk].at[me],
+                send_sem=send_sem.at[chunk, step],
+                recv_sem=recv_sem.at[chunk, step],
+                device_id={"chan": peer(step)},
+                device_id_type=MESH_ID,
+            )
+            copy.start()
+            copies[chunk, step] = copy
+        recv[chunk][me] = send[chunk][me]
+
+    for copy in offs_copies:
+        copy.wait()
+    offs_copy = pltpu.make_async_copy(offs_all, offs_smem, local_sem.at[3])
+    offs_copy.start()
+    offs_copy.wait()
+
+    for position, chunk in enumerate(chunk_order):
+        for step in steps:
+            copies[chunk, step].wait_recv()
+        for block in range(blocks):
+            own = recv[chunk][block].astype(jnp.float32)
+            own_r = own[:, :bins]
+            own_i = own[:, bins:]
+            for slot in range(2):
+                index = jnp.minimum(block + offs_smem[block, 0, slot], blocks - 1)
+                partner = recv[chunk][index].astype(jnp.float32)
+                part_r = partner[:, :bins]
+                part_i = partner[:, bins:]
+                cross_r = own_r * part_r + own_i * part_i
+                cross_i = own_i * part_r - own_r * part_i
+                cross = jnp.concatenate([cross_r, cross_i], axis=1)
+                total = cross[:positions]
+                for seg in range(1, SEGS_PER_CHUNK):
+                    total = total + cross[seg * positions : (seg + 1) * positions]
+                rows = pl.ds(block * positions, positions)
+                if position:
+                    total = total + acc[slot, rows]
+                if position == nchunks - 1:
+                    inside = block + offs_smem[block, 0, slot] < blocks
+                    total = total * jnp.where(inside, 1.0, 0.0).astype(jnp.float32)
+                acc[slot, rows] = total
+
+    other_send[...] = acc[1 - tm].astype(jnp.bfloat16)
+    other_copy = pltpu.make_async_remote_copy(
+        src_ref=other_send,
+        dst_ref=other_recv,
+        send_sem=other_sem.at[0],
+        recv_sem=other_sem.at[1],
+        device_id={"tm": 1 - tm},
+        device_id_type=MESH_ID,
+    )
+    other_copy.start()
+    inverse_copy.wait()
+    for copy in copies.values():
+        copy.wait_send()
+    other_copy.wait()
+    summed = (acc[tm] + other_recv[...].astype(jnp.float32)).astype(jnp.bfloat16)
+    corr = jnp.dot(summed, inverse[...], preferred_element_type=jnp.float32) * scale
+    for block in range(blocks):
+        ret_send[block] = corr[block * positions : (block + 1) * positions]
+    ret_copies = []
+    for step in steps:
+        copy = pltpu.make_async_remote_copy(
+            src_ref=ret_send.at[peer(step)],
+            dst_ref=out_ref.at[me],
+            send_sem=ret_send_sem.at[step],
+            recv_sem=ret_recv_sem.at[step],
+            device_id={"chan": peer(step)},
+            device_id_type=MESH_ID,
+        )
+        copy.start()
+        ret_copies.append(copy)
+    out_ref[me] = ret_send[me]
+
+    @pl.when(tm == 0)
+    def _():
+        hist_copy.wait_send()
+
+    for copy in ret_copies:
+        copy.wait()
+
+
+def exchanged(blocks, strain, taps, offsets, valid):
+    channels, length = strain.shape
+    bins = NFFT // 2
+    segments = length // NFFT
+    positions = channels // blocks
+    nchunks = segments // SEGS_PER_CHUNK
+    scale = 1.0 / math.sqrt(bins * segments * 2)
+    ntaps = taps.shape[0]
+    base = jnp.pad(taps.reshape(1, ntaps), ((0, 0), (0, 256 - ntaps)))
+    offs = jnp.pad(offsets, ((0, 7), (0, 126)))
+    vmem = pl.BlockSpec(memory_space=pltpu.VMEM)
+    hbm = pl.BlockSpec(memory_space=pl.ANY)
+    chunk_buf = pltpu.VMEM((blocks, SEGS_PER_CHUNK * positions, NFFT), jnp.bfloat16)
+    dma = pltpu.SemaphoreType.DMA
+    out = pl.pallas_call(
+        functools.partial(kernel, blocks, scale),
+        out_shape=jax.ShapeDtypeStruct((blocks, positions, LAGS), jnp.float32),
+        in_specs=[hbm, hbm, hbm, vmem, vmem, pl.BlockSpec(memory_space=pltpu.SMEM)],
+        out_specs=vmem,
+        scratch_shapes=[
+            pltpu.VMEM((channels, length), jnp.bfloat16),
+            pltpu.VMEM((NFFT, NFFT), jnp.bfloat16),
+            pltpu.VMEM((NFFT, LAGS), jnp.bfloat16),
+            pltpu.VMEM((channels, 128), jnp.bfloat16),
+            pltpu.VMEM((blocks, 8, 128), jnp.int32),
+            pltpu.SMEM((blocks, 8, 128), jnp.int32),
+            pltpu.VMEM((2, channels, NFFT), jnp.float32),
+            pltpu.VMEM((channels, NFFT), jnp.bfloat16),
+            pltpu.VMEM((channels, NFFT), jnp.bfloat16),
+            pltpu.VMEM((blocks, positions, LAGS), jnp.float32),
+            *[chunk_buf] * (2 * nchunks),
+            dma((4,)),
+            dma((2,)),
+            dma((blocks,)),
+            dma((blocks,)),
+            dma((nchunks, blocks)),
+            dma((nchunks, blocks)),
+            dma((2,)),
+            dma((blocks,)),
+            dma((blocks,)),
+        ],
+        compiler_params=pltpu.CompilerParams(
+            collective_id=0, has_side_effects=True, vmem_limit_bytes=40 * 1024 * 1024
+        ),
+    )(
+        strain,
+        jnp.asarray(host_fourier_table(NFFT, bins)),
+        jnp.asarray(host_lag_table(NFFT, bins, LAGS)),
+        base,
+        offs,
+        valid,
+    )
+    return out.reshape(channels, 1, LAGS)
 
 
 def passed_along(value, axis, steps):
@@ -121,6 +424,10 @@
         P(("groups", "chan")),
     )
     out_specs = P(("groups", "chan"), "tm", None)
+    blocks = mesh.shape["chan"]
+    body = on_device
+    if blocks == 8 and mesh.shape["tm"] == 2:
+        body = functools.partial(exchanged, blocks)
     return jax.shard_map(
-        on_device, mesh=mesh, in_specs=in_specs, out_specs=out_specs, check_vma=False
-    )
+        body, mesh=mesh, in_specs=in_specs, out_specs=out_specs, check_vma=False
+    )

time: 189 us -> 45.9 us (0.24)
  waiting for transfers between devices: 134 us -> 0 us
  Pallas kernels: 0 us -> 38.8 us
  other arithmetic: 17.6 us -> 0 us
  between operations: 16.7 us -> 0.66 us
  matrix products: 7.81 us -> 0 us
  starting transfers between devices: 7.7 us -> 0 us
    ppermute x5 -> x0, waiting for transfers between devices: 133 us -> none  [passed_along(): lax.ppermute(value, axis, [(source, source + steps) for source in range(f...]
    pallas_call x0 -> x1, Pallas kernels: none -> 38.8 us  [exchanged(): pl.pallas_call(functools.partial(kernel, blocks, scale), out_shape=jax.Sh...]
    another operation x9 -> x0, other arithmetic: 11.5 us -> none
    dot_general x5 -> x0, matrix products: 7.81 us -> none  [the longest x1 2.59 us: on_device(): jnp.einsum('csn,nf->scf', frames, fourier_table(fft_len, bins), preferred...]
    ppermute x5 -> x0, starting transfers between devices: 7.7 us -> none  [passed_along(): lax.ppermute(value, axis, [(source, source + steps) for source in range(f...]
    cos x1 -> x0, other arithmetic: 4.12 us -> none  [lag_table(): return jnp.concatenate([jnp.cos(phase), -jnp.sin(phase)], axis=0)]
    unnamed x8 -> x6, local copies, waits for them, and re-layouts: 0.55 us -> 4.04 us
  transfers between devices with their start and end apart: 6 -> 0, of which waited for: 5 -> 0; matrix products, arithmetic and copies ran while one was open for 8% -> 0% of each run, Pallas kernels for 0% -> 0%
where the time goes in v1:
time: 45.9 us; the launch traced here: 45.6 us
  Pallas kernels  38.8 us (85%)
  local copies, waits for them, and re-layouts  6.15 us (13%)
  between operations  0.66 us (1%)
    pallas_call x1, Pallas kernels, exchanged(): pl.pallas_call(functools.partial(kernel, blocks, scale), out_shape=jax.Sh...  38.8 us
    unnamed x6, local copies, waits for them, and re-layouts  4.04 us

profile of v1, /device:TPU:0, one launch (start us, length us, event | category | flops | bytes accessed | tf_op | source)
XLA Modules:
  0.0 45.6 jit_solution(16557200053927809317)
XLA Ops:
  0.7 0.7 %pad.8.taps_ref = f32[1,256]{1,0:T(1,128)S(1)} pad(f32[1,64]{1,0:T(1,128)} %bitcast.3, f32[]{:T(128)} %constant.6.clone.1), padding=0_0x0_192 | pad | bytes 1284 | tf_op jit(solution)/shard_map/jit(_pad)/pad | solution.py:269
  1.3 0.7 %pad.9.offs_ref = s32[8,128]{1,0:T(8,128)S(1)} pad(s32[1,2]{1,0:T(1,128)} %param.8, s32[]{:T(128)} %constant.7.clone.1), padding=0_7x0_126 | pad | bytes 4108 | tf_op jit(solution)/shard_map/jit(_pad)/pad | solution.py:270
  2.0 0.0 copy-start
  2.0 1.6 %copy-done = bf16[1024,1024]{1,0:T(8,128)(2,1)S(1)} copy-done((bf16[1024,1024]{1,0:T(8,128)(2,1)S(1)}, bf16[1024,1024]{1,0:T(8,128)(2,1)}, u32[]{:S(2)}) %copy-start) | copy-done | bytes 2097176
  3.6 0.0 copy-start.1
  3.6 1.2 %copy-done.1 = bf16[64,8192]{1,0:T(8,128)(2,1)S(1)} copy-done((bf16[64,8192]{1,0:T(8,128)(2,1)S(1)}, bf16[64,8192]{1,0:T(8,128)(2,1)}, u32[]{:S(2)}) %copy-start.1) | copy-done | bytes 1048600
  4.8 0.0 copy-start.2
  4.8 1.2 %copy-done.2 = bf16[1024,512]{1,0:T(8,128)(2,1)S(1)} copy-done((bf16[1024,512]{1,0:T(8,128)(2,1)S(1)}, bf16[1024,512]{1,0:T(8,128)(2,1)}, u32[]{:S(2)}) %copy-start.2) | copy-done | bytes 1048600
  6.0 38.8 %shard_map.64 = f32[8,8,512]{2,1,0:T(8,128)S(1)} custom-call(bf16[64,8192]{1,0:T(8,128)(2,1)S(1)} %copy-done.1, bf16[1024,1024]{1,0:T(8,128)(2,1)S(1)} %copy-done, bf16[1024,512]{1,0:T(8,128)(2,1)S(1)} %copy-done.2, f32[1,256]{1,0:T(1,128)S(1)} %pad.8.taps_ref, s32[8,128]{1,0:T(8,128)S(1)} %pad.9.offs_ref, s32[1]{0:T(128)S(6)} %copy.8.valid_ref), custom_call_target="tpu_custom_call" | custom-call | tf_op jit(solution)/shard_map/pallas_call | solution.py:275
  44.8 0.8 %copy.7 = f32[64,1,512]{2,1,0:T(1,128)} copy(f32[64,1,512]{2,0,1:T(8,128)S(1)} %bitcast.2) | data formatting | bytes 262144 | tf_op jit(solution)/shard_map/reshape | solution.py:313
Async XLA Ops:
  2.0 1.6 %copy-start = (bf16[1024,1024]{1,0:T(8,128)(2,1)S(1)}, bf16[1024,1024]{1,0:T(8,128)(2,1)}, u32[]{:S(2)}) copy-start(bf16[1024,1024]{1,0:T(8,128)(2,1)} %constant.8.clone.table_hbm) | copy-start | bytes 6291460
  3.6 1.2 %copy-start.1 = (bf16[64,8192]{1,0:T(8,128)(2,1)S(1)}, bf16[64,8192]{1,0:T(8,128)(2,1)}, u32[]{:S(2)}) copy-start(bf16[64,8192]{1,0:T(8,128)(2,1)} %strain_hbm.1) | copy-start | bytes 3145732
  4.8 1.2 %copy-start.2 = (bf16[1024,512]{1,0:T(8,128)(2,1)S(1)}, bf16[1024,512]{1,0:T(8,128)(2,1)}, u32[]{:S(2)}) copy-start(bf16[1024,512]{1,0:T(8,128)(2,1)} %constant.9.clone.inverse_hbm) | copy-start | bytes 3145732

commit v2 on v1

--- a/solution.py
+++ b/solution.py
@@ -44,12 +44,14 @@
     table,
     inverse,
     history,
-    offs_all,
-    offs_smem,
+    base,
+    info,
+    info_all,
+    info_smem,
     acc,
-    other_send,
-    other_recv,
+    white_first,
     ret_send,
+    ret_recv,
     *rest,
 ):
     channels, length = strain.shape
@@ -58,17 +60,28 @@
     segments = length // fft_len
     nchunks = segments // SEGS_PER_CHUNK
     positions = channels // blocks
+    ntaps = taps_ref.shape[1]
     send = rest[:nchunks]
     recv = rest[nchunks : 2 * nchunks]
-    (local_sem, hist_sem, offs_send_sem, offs_recv_sem, send_sem, recv_sem, other_sem,
+    (local_sem, hist_sem, info_send_sem, info_recv_sem, send_sem, recv_sem,
      ret_send_sem, ret_recv_sem) = rest[2 * nchunks :]
 
     me = lax.axis_index("chan")
     tm = lax.axis_index("tm")
     steps = range(1, blocks)
+    ret_steps = [(step, flip) for step in range(blocks) for flip in range(2) if step or flip]
 
     def peer(step):
         return lax.rem(me + step, blocks)
+
+    def core(flip):
+        return 1 - tm if flip else tm
+
+    barrier = pltpu.get_barrier_semaphore()
+    for step, flip in ret_steps:
+        pl.semaphore_signal(
+            barrier, inc=1, device_id={"chan": peer(step), "tm": core(flip)}, device_id_type=MESH_ID
+        )
 
     strain_copy = pltpu.make_async_copy(strain_hbm, strain, local_sem.at[0])
     table_copy = pltpu.make_async_copy(table_hbm, table, local_sem.at[1])
@@ -77,102 +90,66 @@
     table_copy.start()
     inverse_copy.start()
 
-    barrier = pltpu.get_barrier_semaphore()
-    for step in steps:
-        pl.semaphore_signal(barrier, inc=1, device_id={"chan": peer(step)}, device_id_type=MESH_ID)
-    pl.semaphore_signal(barrier, inc=1, device_id={"tm": 1 - tm}, device_id_type=MESH_ID)
-
-    base = jnp.broadcast_to(taps_ref[...], (256, 256))
-    fir_full = pltpu.roll(base, 128, 1, stride=1, stride_axis=0)[:, :128]
+    base[...] = jnp.zeros_like(base)
+    base[:, :ntaps] = taps_ref[...]
+    fir_full = pltpu.roll(
+        jnp.broadcast_to(base[...], (256, 256)), 128, 1, stride=1, stride_axis=0
+    )[:, :128]
     fir_high = fir_full.astype(jnp.bfloat16)
     fir_low = (fir_full - fir_high.astype(jnp.float32)).astype(jnp.bfloat16)
     fir = jnp.concatenate([fir_high, fir_low], axis=1)
 
-    pl.semaphore_wait(barrier, blocks)
-    strain_copy.wait()
-
-    hist_copy = pltpu.make_async_remote_copy(
-        src_ref=strain.at[:, length - 128 :],
-        dst_ref=history,
-        send_sem=hist_sem.at[0],
-        recv_sem=hist_sem.at[1],
-        device_id={"tm": 1 - tm},
-        device_id_type=MESH_ID,
-    )
-
-    @pl.when(tm == 0)
-    def _():
-        hist_copy.start()
-        history[...] = jnp.zeros_like(history)
-
-    offs_copies = []
-    for step in steps:
-        copy = pltpu.make_async_remote_copy(
-            src_ref=offs_ref,
-            dst_ref=offs_all.at[me],
-            send_sem=offs_send_sem.at[step],
-            recv_sem=offs_recv_sem.at[step],
-            device_id={"chan": peer(step)},
-            device_id_type=MESH_ID,
-        )
-        copy.start()
-        offs_copies.append(copy)
-    offs_all[me] = offs_ref[...]
-
-    table_copy.wait()
+    lane = lax.broadcasted_iota(jnp.int32, info.shape, 1)
+    info[...] = jnp.where(
+        lane == 0, offs_ref[0, 0], jnp.where(lane == 1, offs_ref[0, 1], valid_ref[0])
+    )
     live = lax.broadcasted_iota(jnp.int32, (channels, 1), 0) < valid_ref[0]
     live = jnp.where(live, 1.0, 0.0).astype(jnp.float32)
     live = jnp.concatenate([live] * SEGS_PER_CHUNK, axis=0)
 
-    chunk_order = list(range(1, nchunks)) + [0]
-    copies = {}
-    for chunk in chunk_order:
+    def filtered_frames(chunk):
         first = chunk * SEGS_PER_CHUNK
         windows = []
         for j in range(first * 8, (first + SEGS_PER_CHUNK) * 8):
             if j == 0:
-
-                @pl.when(tm == 1)
-                def _():
-                    hist_copy.wait_recv()
-
                 windows.append(jnp.concatenate([history[...], strain[:, :128]], axis=1))
             else:
                 windows.append(strain[:, 128 * (j - 1) : 128 * (j + 1)])
         window = jnp.concatenate(windows, axis=0)
         both = jnp.dot(window, fir, preferred_element_type=jnp.float32)
-        rounded = (both[:, :128] + both[:, 128:]).astype(jnp.bfloat16)
-        frames = jnp.concatenate(
+        flat = both[:, :128] + both[:, 128:]
+        return jnp.concatenate(
             [
                 jnp.concatenate(
-                    [
-                        rounded[(seg * 8 + j) * channels : (seg * 8 + j + 1) * channels]
-                        for j in range(8)
-                    ],
-                    axis=1,
+                    [flat[(seg * 8 + j) * channels :][:channels] for j in range(8)], axis=1
                 )
                 for seg in range(SEGS_PER_CHUNK)
             ],
             axis=0,
         )
+
+    def whitened(frames, row_live):
         spectra = jnp.dot(frames, table[...], preferred_element_type=jnp.float32)
         real_part = spectra[:, :bins]
         imag_part = spectra[:, bins:]
         energy = real_part * real_part + imag_part * imag_part
         power = jnp.mean(energy, axis=1, keepdims=True) + 1e-06
-        factor = live * lax.rsqrt(energy + 0.1 * power)
-        white_r = real_part * factor
-        white_i = imag_part * factor
-        for block in range(blocks):
-            for part, half in ((white_r, 0), (white_i, 1)):
-                rows = jnp.concatenate(
-                    [
-                        part[seg * channels + block * positions :][:positions]
-                        for seg in range(SEGS_PER_CHUNK)
-                    ],
-                    axis=0,
-                )
-                send[chunk][block, :, half * bins : (half + 1) * bins] = rows.astype(jnp.bfloat16)
+        factor = row_live * lax.rsqrt(energy + 0.1 * power)
+        return real_part * factor, imag_part * factor
+
+    def by_block(part, block):
+        return jnp.concatenate(
+            [
+                part[seg * channels + block * positions :][:positions]
+                for seg in range(SEGS_PER_CHUNK)
+            ],
+            axis=0,
+        ).astype(jnp.bfloat16)
+
+    chunk_order = list(range(1, nchunks)) + [0]
+    copies = {}
+
+    def send_chunk(chunk):
         for step in steps:
             copy = pltpu.make_async_remote_copy(
                 src_ref=send[chunk].at[peer(step)],
@@ -186,22 +163,88 @@
             copies[chunk, step] = copy
         recv[chunk][me] = send[chunk][me]
 
-    for copy in offs_copies:
+    opening = chunk_order[0]
+    strain_copy.wait()
+    frames = filtered_frames(opening)
+    for block in range(blocks):
+        send[opening][block] = by_block(frames, block)
+
+    pl.semaphore_wait(barrier, len(ret_steps))
+    send_chunk(opening)
+
+    hist_copy = pltpu.make_async_remote_copy(
+        src_ref=strain.at[:, length - 128 :],
+        dst_ref=history,
+        send_sem=hist_sem.at[0],
+        recv_sem=hist_sem.at[1],
+        device_id={"tm": 1 - tm},
+        device_id_type=MESH_ID,
+    )
+
+    @pl.when(tm == 0)
+    def _():
+        hist_copy.start()
+        history[...] = jnp.zeros_like(history)
+
+    info_copies = []
+    for step in steps:
+        copy = pltpu.make_async_remote_copy(
+            src_ref=info,
+            dst_ref=info_all.at[me],
+            send_sem=info_send_sem.at[step],
+            recv_sem=info_recv_sem.at[step],
+            device_id={"chan": peer(step)},
+            device_id_type=MESH_ID,
+        )
+        copy.start()
+        info_copies.append(copy)
+    info_all[me] = info[...]
+
+    table_copy.wait()
+    for chunk in chunk_order[1:]:
+        if chunk == 0:
+
+            @pl.when(tm == 1)
+            def _():
+                hist_copy.wait_recv()
+
+        frames = filtered_frames(chunk).astype(jnp.bfloat16)
+        white_r, white_i = whitened(frames, live)
+        for block in range(blocks):
+            send[chunk][block, :, :bins] = by_block(white_r, block)
+            send[chunk][block, :, bins:] = by_block(white_i, block)
+        send_chunk(chunk)
+
+    for copy in info_copies:
         copy.wait()
-    offs_copy = pltpu.make_async_copy(offs_all, offs_smem, local_sem.at[3])
-    offs_copy.start()
-    offs_copy.wait()
+    info_copy = pltpu.make_async_copy(info_all, info_smem, local_sem.at[3])
+    info_copy.start()
+    info_copy.wait()
 
     for position, chunk in enumerate(chunk_order):
         for step in steps:
             copies[chunk, step].wait_recv()
+        panel = recv[chunk]
+        if chunk == opening:
+            index = lax.broadcasted_iota(jnp.int32, (positions, 1), 0) + me * positions
+            row_live = []
+            for block in range(blocks):
+                alive = jnp.where(index < info_smem[block, 0, 2], 1.0, 0.0).astype(jnp.float32)
+                row_live.extend([alive] * SEGS_PER_CHUNK)
+            frames = jnp.concatenate([panel[block] for block in range(blocks)], axis=0)
+            white_r, white_i = whitened(frames, jnp.concatenate(row_live, axis=0))
+            panel = white_first
+            rows = SEGS_PER_CHUNK * positions
+            for block in range(blocks):
+                panel[block, :, :bins] = white_r[block * rows :][:rows].astype(jnp.bfloat16)
+                panel[block, :, bins:] = white_i[block * rows :][:rows].astype(jnp.bfloat16)
         for block in range(blocks):
-            own = recv[chunk][block].astype(jnp.float32)
+            own = panel[block].astype(jnp.float32)
             own_r = own[:, :bins]
             own_i = own[:, bins:]
             for slot in range(2):
-                index = jnp.minimum(block + offs_smem[block, 0, slot], blocks - 1)
-                partner = recv[chunk][index].astype(jnp.float32)
+                index = jnp.minimum(block + info_smem[block, 0, slot], blocks - 1)
+                partner = panel[index].astype(jnp.float32)
                 part_r = partner[:, :bins]
                 part_i = partner[:, bins:]
                 cross_r = own_r * part_r + own_i * part_i
@@ -210,52 +253,51 @@
                 total = cross[:positions]
                 for seg in range(1, SEGS_PER_CHUNK):
                     total = total + cross[seg * positions : (seg + 1) * positions]
-                rows = pl.ds(block * positions, positions)
+                rows = pl.ds(slot * channels + block * positions, positions)
                 if position:
-                    total = total + acc[slot, rows]
+                    total = total + acc[rows]
                 if position == nchunks - 1:
-                    inside = block + offs_smem[block, 0, slot] < blocks
-                    total = total * jnp.where(inside, 1.0, 0.0).astype(jnp.float32)
-                acc[slot, rows] = total
-
-    other_send[...] = acc[1 - tm].astype(jnp.bfloat16)
-    other_copy = pltpu.make_async_remote_copy(
-        src_ref=other_send,
-        dst_ref=other_recv,
-        send_sem=other_sem.at[0],
-        recv_sem=other_sem.at[1],
-        device_id={"tm": 1 - tm},
-        device_id_type=MESH_ID,
-    )
-    other_copy.start()
-    inverse_copy.wait()
-    for copy in copies.values():
-        copy.wait_send()
-    other_copy.wait()
-    summed = (acc[tm] + other_recv[...].astype(jnp.float32)).astype(jnp.bfloat16)
-    corr = jnp.dot(summed, inverse[...], preferred_element_type=jnp.float32) * scale
-    for block in range(blocks):
-        ret_send[block] = corr[block * positions : (block + 1) * positions]
+                    inside = block + info_smem[block, 0, slot] < blocks
+                    total = total * jnp.where(inside, scale, 0.0).astype(jnp.float32)
+                acc[rows] = total
+        if position == 0:
+            inverse_copy.wait()
+
+    corr = jnp.dot(
+        acc[...].astype(jnp.bfloat16), inverse[...], preferred_element_type=jnp.float32
+    )
+    half = corr.shape[1] // 2
+    for slot in range(2):
+        for block in range(blocks):
+            rows = corr[slot * channels + block * positions :][:positions]
+            rows = jnp.concatenate([rows[:, :half], rows[:, half:]], axis=0)
+            ret_send[slot, block] = rows.astype(jnp.bfloat16)
     ret_copies = []
-    for step in steps:
+    for step, flip in ret_steps:
         copy = pltpu.make_async_remote_copy(
-            src_ref=ret_send.at[peer(step)],
-            dst_ref=out_ref.at[me],
-            send_sem=ret_send_sem.at[step],
-            recv_sem=ret_recv_sem.at[step],
-            device_id={"chan": peer(step)},
+            src_ref=ret_send.at[core(flip), peer(step)],
+            dst_ref=ret_recv.at[tm, me],
+            send_sem=ret_send_sem.at[step, flip],
+            recv_sem=ret_recv_sem.at[step, flip],
+            device_id={"chan": peer(step), "tm": core(flip)},
             device_id_type=MESH_ID,
         )
         copy.start()
         ret_copies.append(copy)
-    out_ref[me] = ret_send[me]
+    ret_recv[tm, me] = ret_send[tm, me]
 
     @pl.when(tm == 0)
     def _():
         hist_copy.wait_send()
 
+    for copy in copies.values():
+        copy.wait_send()
     for copy in ret_copies:
         copy.wait()
+    for block in range(blocks):
+        rows = ret_recv[0, block].astype(jnp.float32) + ret_recv[1, block].astype(jnp.float32)
+        out_ref[block, :, :half] = rows[:positions]
+        out_ref[block, :, half:] = rows[positions:]
 
 
 def exchanged(blocks, strain, taps, offsets, valid):
@@ -265,29 +307,30 @@
     positions = channels // blocks
     nchunks = segments // SEGS_PER_CHUNK
     scale = 1.0 / math.sqrt(bins * segments * 2)
-    ntaps = taps.shape[0]
-    base = jnp.pad(taps.reshape(1, ntaps), ((0, 0), (0, 256 - ntaps)))
-    offs = jnp.pad(offsets, ((0, 7), (0, 126)))
     vmem = pl.BlockSpec(memory_space=pltpu.VMEM)
+    smem = pl.BlockSpec(memory_space=pltpu.SMEM)
     hbm = pl.BlockSpec(memory_space=pl.ANY)
     chunk_buf = pltpu.VMEM((blocks, SEGS_PER_CHUNK * positions, NFFT), jnp.bfloat16)
+    ret_buf = pltpu.VMEM((2, blocks, 2 * positions, LAGS // 2), jnp.bfloat16)
     dma = pltpu.SemaphoreType.DMA
     out = pl.pallas_call(
         functools.partial(kernel, blocks, scale),
         out_shape=jax.ShapeDtypeStruct((blocks, positions, LAGS), jnp.float32),
-        in_specs=[hbm, hbm, hbm, vmem, vmem, pl.BlockSpec(memory_space=pltpu.SMEM)],
+        in_specs=[hbm, hbm, hbm, vmem, smem, smem],
         out_specs=vmem,
         scratch_shapes=[
             pltpu.VMEM((channels, length), jnp.bfloat16),
             pltpu.VMEM((NFFT, NFFT), jnp.bfloat16),
             pltpu.VMEM((NFFT, LAGS), jnp.bfloat16),
             pltpu.VMEM((channels, 128), jnp.bfloat16),
+            pltpu.VMEM((1, 256), jnp.float32),
+            pltpu.VMEM((8, 128), jnp.int32),
             pltpu.VMEM((blocks, 8, 128), jnp.int32),
             pltpu.SMEM((blocks, 8, 128), jnp.int32),
-            pltpu.VMEM((2, channels, NFFT), jnp.float32),
-            pltpu.VMEM((channels, NFFT), jnp.bfloat16),
-            pltpu.VMEM((channels, NFFT), jnp.bfloat16),
-            pltpu.VMEM((blocks, positions, LAGS), jnp.float32),
+            pltpu.VMEM((2 * channels, NFFT), jnp.float32),
+            chunk_buf,
+            ret_buf,
+            ret_buf,
             *[chunk_buf] * (2 * nchunks),
             dma((4,)),
             dma((2,)),
@@ -295,19 +338,18 @@
             dma((blocks,)),
             dma((nchunks, blocks)),
             dma((nchunks, blocks)),
-            dma((2,)),
-            dma((blocks,)),
-            dma((blocks,)),
+            dma((blocks, 2)),
+            dma((blocks, 2)),
         ],
         compiler_params=pltpu.CompilerParams(
-            collective_id=0, has_side_effects=True, vmem_limit_bytes=40 * 1024 * 1024
+            collective_id=0, has_side_effects=True, vmem_limit_bytes=60 * 1024 * 1024
         ),
     )(
         strain,
         jnp.asarray(host_fourier_table(NFFT, bins)),
         jnp.asarray(host_lag_table(NFFT, bins, LAGS)),
-        base,
-        offs,
+        taps.reshape(1, -1),
+        offsets,
         valid,
     )
     return out.reshape(channels, 1, LAGS)

time: 45.9 us -> 41.3 us (0.90)
  local copies, waits for them, and re-layouts: 6.15 us -> 1.69 us
    unnamed x6 -> x0, local copies, waits for them, and re-layouts: 4.04 us -> none
    pad x2 -> x0, local copies, waits for them, and re-layouts: 1.32 us -> none  [the longest x1 0.66 us: exchanged(): base = jnp.pad(taps.reshape(1, ntaps), ((0, 0), (0, 256 - ntaps)))]
    reshape x1, local copies, waits for them, and re-layouts: 0.79 us -> 1.69 us  [exchanged(): return out.reshape(channels, 1, LAGS)]
where the time goes in v2:
time: 41.3 us; the launch traced here: 41.1 us
  Pallas kernels  38.8 us (94%)
  local copies, waits for them, and re-layouts  1.69 us (4%)
  between operations  0.66 us (2%)
    pallas_call x1, Pallas kernels, exchanged(): pl.pallas_call(functools.partial(kernel, blocks, scale), out_shape=jax.Sh...  38.8 us
    reshape x1, local copies, waits for them, and re-layouts, exchanged(): return out.reshape(channels, 1, LAGS)  1.69 us

profile of v2, /device:TPU:0, one launch (start us, length us, event | category | flops | bytes accessed | tf_op | source)
XLA Modules:
  0.0 41.1 jit_solution(3471047910908279803)
XLA Ops:
  0.7 38.8 %shard_map.64 = f32[8,8,512]{2,1,0:T(8,128)} custom-call(bf16[64,8192]{1,0:T(8,128)(2,1)} %strain_hbm.1, bf16[1024,1024]{1,0:T(8,128)(2,1)} %constant.4.clone.table_hbm, bf16[1024,512]{1,0:T(8,128)(2,1)} %constant.5.clone.inverse_hbm, f32[1,64]{1,0:T(1,128)} %bitcast.3, s32[1,2]{1,0:T(1,128)} %offs_ref.1, s32[1]{0:T(128)S(6)} %copy.8.valid_ref), custom_call_target="tpu_custom_call" | custom-call | tf_op jit(solution)/shard_map/pallas_call | solution.py:316
  39.4 1.7 %copy.7 = f32[64,1,512]{2,1,0:T(1,128)} copy(f32[64,1,512]{2,0,1:T(8,128)} %bitcast.2) | data formatting | bytes 262144 | tf_op jit(solution)/shard_map/reshape | solution.py:355

commit v3 on v2

--- a/solution.py
+++ b/solution.py
@@ -68,11 +68,11 @@
 
     me = lax.axis_index("chan")
     tm = lax.axis_index("tm")
-    steps = range(1, blocks)
-    ret_steps = [(step, flip) for step in range(blocks) for flip in range(2) if step or flip]
+    steps = (7, 6, 5, 4, 3, 2, 1)
+    ret_steps = [(step, flip) for step in range(blocks - 1, -1, -1) for flip in range(2) if step or flip]
 
     def peer(step):
-        return lax.rem(me + step, blocks)
+        return me ^ step
 
     def core(flip):
         return 1 - tm if flip else tm

time: 41.3 us -> 40.8 us (0.988)
  Pallas kernels: 38.8 us -> 38.3 us
    pallas_call x1, Pallas kernels: 38.8 us -> 38.3 us  [exchanged(): pl.pallas_call(functools.partial(kernel, blocks, scale), out_shape=jax.Sh...]
where the time goes in v3:
time: 40.8 us; the launch traced here: 40.7 us
  Pallas kernels  38.3 us (94%)
  local copies, waits for them, and re-layouts  1.69 us (4%)
  between operations  0.66 us (2%)
    pallas_call x1, Pallas kernels, exchanged(): pl.pallas_call(functools.partial(kernel, blocks, scale), out_shape=jax.Sh...  38.3 us
    reshape x1, local copies, waits for them, and re-layouts, exchanged(): return out.reshape(channels, 1, LAGS)  1.69 us

profile of v3, /device:TPU:0, one launch (start us, length us, event | category | flops | bytes accessed | tf_op | source)
XLA Modules:
  0.0 40.7 jit_solution(219083253775924466)
XLA Ops:
  0.7 38.3 %shard_map.64 = f32[8,8,512]{2,1,0:T(8,128)} custom-call(bf16[64,8192]{1,0:T(8,128)(2,1)} %strain_hbm.1, bf16[1024,1024]{1,0:T(8,128)(2,1)} %constant.4.clone.table_hbm, bf16[1024,512]{1,0:T(8,128)(2,1)} %constant.5.clone.inverse_hbm, f32[1,64]{1,0:T(1,128)} %bitcast.3, s32[1,2]{1,0:T(1,128)} %offs_ref.1, s32[1]{0:T(128)S(6)} %copy.8.valid_ref), custom_call_target="tpu_custom_call" | custom-call | tf_op jit(solution)/shard_map/pallas_call | solution.py:316
  39.0 1.7 %copy.7 = f32[64,1,512]{2,1,0:T(1,128)} copy(f32[64,1,512]{2,0,1:T(8,128)} %bitcast.2) | data formatting | bytes 262144 | tf_op jit(solution)/shard_map/reshape | solution.py:355
